TPU v7x, 32 devices: a whole 2x2x4 slice. The times are simulated.
32 devices in a mesh: noise: 8 (over z, y), dp: 4 (over x, core).
Axes of the slice: x: 2, y: 2, z: 4, core: 2. Of those that a mesh axis runs over, the one named last changes fastest.
Arguments:
- noise_latents: bfloat16 [2048, 2048], P(('noise', 'dp')), may hold values from -7 to 7
- data_latents: bfloat16 [8192, 2048], P(('dp', 'noise')), may hold values from -16 to 16
Outputs:
- paired_target: bfloat16 [2048, 2048], P('noise', 'dp')
- noise_potential: float32 [2048], P('noise')
- data_potential: float32 [8192], P('dp')
All inputs are finite; a program needn't handle non-finite values.
Results may differ from a plain program's by a relative error of at most 0.0046.
Values may be sent and summed in bfloat16 or wider, within the bound.
A program may use at most 64 MiB of HBM per device.

v0:
```python
import jax
import jax.numpy as jnp
from jax import lax
from jax.sharding import PartitionSpec as P

ITERS = 3


smoothing = 0.05


def merged(part, axis, combine):
    gathered = jax.tree.map(lambda a: lax.all_gather(a, axis), part)

    def take(source):
        return jax.tree.map(lambda a: lax.dynamic_index_in_dim(a, source, 0, False), gathered)

    return lax.fori_loop(
        1, lax.axis_size(axis), lambda source, state: combine(state, take(source)), take(0)
    )


def combine_stats(first, second):
    top = jnp.maximum(first[0], second[0])
    total = first[1] * jnp.exp(first[0] - top) + second[1] * jnp.exp(second[0] - top)
    return (top, total)


def row_stats(cost, data_potential):
    scores = (data_potential[None, :] - cost) / smoothing
    local_top = jnp.max(scores, axis=1)
    local_sum = jnp.sum(jnp.exp(scores - local_top[:, None]), axis=1)
    top, total = merged((local_top, local_sum), "dp", combine_stats)
    return (scores, top, total)


def column_lse(cost, noise_potential):
    scores = (noise_potential[:, None] - cost) / smoothing
    local_top = jnp.max(scores, axis=0)
    top = lax.pmax(local_top, "noise")
    total = lax.psum(jnp.sum(jnp.exp(scores - top[None, :]), axis=0), "noise")
    return jnp.log(total) + top


def local(noise_latents, data_latents):
    rows = lax.all_gather(noise_latents, "dp", axis=0, tiled=True)
    width = rows.shape[1]
    total_rows = rows.shape[0] * lax.axis_size("noise")
    row_norms = jnp.sum(jnp.square(rows.astype(jnp.float32)), axis=1)
    block = lax.all_gather(data_latents, "noise", axis=0, tiled=True)
    piece_norms = jnp.sum(jnp.square(block.astype(jnp.float32)), axis=1)
    inner = jnp.dot(rows, block.T, preferred_element_type=jnp.float32)
    cost = (row_norms[:, None] + piece_norms[None, :] - 2.0 * inner) / width
    total_cols = cost.shape[1] * lax.axis_size("dp")
    data_potential = jnp.zeros((cost.shape[1],), jnp.float32)
    noise_potential = jnp.zeros((cost.shape[0],), jnp.float32)
    for step in range(ITERS):
        scores, top, total = row_stats(cost, data_potential)
        noise_potential = -smoothing * jnp.log(jnp.float32(total_rows)) - smoothing * (
            jnp.log(total) + top
        )
        data_potential = -smoothing * jnp.log(jnp.float32(total_cols)) - smoothing * column_lse(
            cost, noise_potential
        )
    scores, top, total = row_stats(cost, data_potential)
    weights = (jnp.exp(scores - top[:, None]) / total[:, None]).astype(jnp.bfloat16)
    partial_sum = jnp.dot(weights, block, preferred_element_type=jnp.float32)
    paired_target = lax.psum_scatter(partial_sum, "dp", scatter_dimension=1, tiled=True).astype(
        jnp.bfloat16
    )
    return (paired_target, noise_potential, data_potential)


def solution(mesh):
    placed = (P(("noise", "dp"), None), P(("dp", "noise"), None))
    return jax.shard_map(
        local,
        mesh=mesh,
        in_specs=placed,
        out_specs=(P("noise", "dp"), P("noise"), P("dp")),
        check_vma=False,
    )
```

profile of v0, /device:TPU:0, one launch (start us, length us, event | category | flops | bytes accessed | tf_op | source)
XLA Modules:
  0.0 367.0 jit_solution(13718602900019240198)
XLA Ops:
  7.2 0.0 all-gather.19.cloned.1.call-start
  7.2 0.7 all-gather.19.cloned.1.call-update
  7.9 0.0 all-gather.21.cloned.1.call-start
  7.9 0.7 all-gather.21.cloned.1.call-update
  8.6 0.0 reduce-scatter.2.cloned.1.call-start
  8.7 20.3 %all-gather.19.cloned.1.call-done = bf16[256,2048]{1,0:T(8,128)(2,1)} async-done(((bf16[64,2048]{1,0:T(8,128)(2,1)}), bf16[256,2048]{1,0:T(8,128)(2,1)}) %all-gather.19.cloned.1.call-update) | async-done | bytes 1048592 | tf_op jit(solution)/shard_map/all_gather | solution.py:46
  29.0 0.0 copy-start.1
  29.0 1.6 multiply_reduce_fusion.1
  30.6 125.5 %all-gather.21.cloned.1.call-done = bf16[2048,2048]{1,0:T(8,128)(2,1)} async-done(((bf16[256,2048]{1,0:T(8,128)(2,1)}), bf16[2048,2048]{1,0:T(8,128)(2,1)}) %all-gather.21.cloned.1.call-update) | async-done | bytes 8388624 | tf_op jit(solution)/shard_map/all_gather | solution.py:50
  156.1 0.0 copy-start
  156.1 5.2 %multiply_reduce_fusion = f32[2048]{0:T(1024)S(1)} fusion(bf16[2048,2048]{1,0:T(8,128)(2,1)} %all-gather.21.cloned.1.call-done), kind=kLoop, calls=%fused_computation.12 | loop fusion | flops 12580864 | bytes 8396800 | tf_op jit(solution)/shard_map/reduce_sum | solution.py:51
  161.3 0.0 copy-done.1
  161.4 0.5 copy-done
  161.9 3.0 fusion.2
  164.8 0.5 exponential_reduce_fusion.6
  165.4 5.1 %all-gather.9 = f32[4,1,256]{2,1,0:T(1,128)S(1)} all-gather(f32[1,1,256]{2,1,0:T(1,128)S(1)} %bitcast.97), channel_id=3, replica_groups=mesh['noise'=8,'dp'=4] {'dp'}, dimensions={0}, use_global_device_ids=true | all-gather | bytes 5120 | tf_op jit(solution)/shard_map/all_gather | solution.py:13
  170.5 5.1 %all-gather.8 = f32[4,1,256]{2,1,0:T(1,128)S(1)} all-gather(f32[1,1,256]{2,1,0:T(1,128)S(1)} %bitcast.94), channel_id=2, replica_groups=mesh['noise'=8,'dp'=4] {'dp'}, dimensions={0}, use_global_device_ids=true | all-gather | bytes 5120 | tf_op jit(solution)/shard_map/all_gather | solution.py:13
  175.5 0.1 while.68
  175.7 0.3 fusion.3
  176.0 18.7 %pmax.21 = f32[2048]{0:T(1024)S(1)} all-reduce(f32[2048]{0:T(1024)S(1)} %fusion.3), channel_id=1, replica_groups=mesh['noise'=8,'dp'=4] {'noise'}, use_global_device_ids=true, to_apply=%region_7.8 | all-reduce | flops 2048 | bytes 16384 | tf_op jit(solution)/shard_map/pmax | solution.py:40
  194.6 0.5 exponential_reduce_fusion.5
  195.1 18.1 %psum.21 = f32[2048]{0:T(1024)S(1)} all-reduce(f32[2048]{0:T(1024)S(1)} %exponential_reduce_fusion.5), channel_id=1, replica_groups=mesh['noise'=8,'dp'=4] {'noise'}, use_global_device_ids=true, to_apply=%region_9.10 | all-reduce | flops 2048 | bytes 16384 | tf_op jit(solution)/shard_map/psum | solution.py:41
  213.3 0.3 fusion.4
  213.6 0.5 exponential_reduce_fusion.4
  214.1 5.1 %all-gather.10 = f32[4,1,256]{2,1,0:T(1,128)S(1)} all-gather(f32[1,1,256]{2,1,0:T(1,128)S(1)} %bitcast.92), channel_id=4, replica_groups=mesh['noise'=8,'dp'=4] {'dp'}, dimensions={0}, use_global_device_ids=true | all-gather | bytes 5120 | tf_op jit(solution)/shard_map/all_gather | solution.py:13
  219.2 5.1 %all-gather.11 = f32[4,1,256]{2,1,0:T(1,128)S(1)} all-gather(f32[1,1,256]{2,1,0:T(1,128)S(1)} %bitcast.95), channel_id=5, replica_groups=mesh['noise'=8,'dp'=4] {'dp'}, dimensions={0}, use_global_device_ids=true | all-gather | bytes 5120 | tf_op jit(solution)/shard_map/all_gather | solution.py:13
  224.2 0.1 while.69
  224.4 0.3 fusion.5
  224.7 18.7 %pmax.22 = f32[2048]{0:T(1024)S(1)} all-reduce(f32[2048]{0:T(1024)S(1)} %fusion.5), channel_id=1, replica_groups=mesh['noise'=8,'dp'=4] {'noise'}, use_global_device_ids=true, to_apply=%region_15.16 | all-reduce | flops 2048 | bytes 16384 | tf_op jit(solution)/shard_map/pmax | solution.py:40
  243.4 0.5 exponential_reduce_fusion.3
  243.9 18.0 %psum.22 = f32[2048]{0:T(1024)S(1)} all-reduce(f32[2048]{0:T(1024)S(1)} %exponential_reduce_fusion.3), channel_id=1, replica_groups=mesh['noise'=8,'dp'=4] {'noise'}, use_global_device_ids=true, to_apply=%region_17.18 | all-reduce | flops 2048 | bytes 16384 | tf_op jit(solution)/shard_map/psum | solution.py:41
  262.0 0.3 fusion.6
  262.3 0.5 exponential_reduce_fusion.2
  262.8 5.1 %all-gather.12 = f32[4,1,256]{2,1,0:T(1,128)S(1)} all-gather(f32[1,1,256]{2,1,0:T(1,128)S(1)} %bitcast.93), channel_id=6, replica_groups=mesh['noise'=8,'dp'=4] {'dp'}, dimensions={0}, use_global_device_ids=true | all-gather | bytes 5120 | tf_op jit(solution)/shard_map/all_gather | solution.py:13
  267.9 5.1 %all-gather.13 = f32[4,1,256]{2,1,0:T(1,128)S(1)} all-gather(f32[1,1,256]{2,1,0:T(1,128)S(1)} %bitcast.96), channel_id=7, replica_groups=mesh['noise'=8,'dp'=4] {'dp'}, dimensions={0}, use_global_device_ids=true | all-gather | bytes 5120 | tf_op jit(solution)/shard_map/all_gather | solution.py:13
  273.0 0.1 while.70
  273.1 0.0 copy-start.3
  273.1 0.3 fusion.7
  273.4 18.7 %pmax.23 = f32[2048]{0:T(1024)S(1)} all-reduce(f32[2048]{0:T(1024)S(1)} %fusion.7), channel_id=1, replica_groups=mesh['noise'=8,'dp'=4] {'noise'}, use_global_device_ids=true, to_apply=%region_23.24 | all-reduce | flops 2048 | bytes 16384 | tf_op jit(solution)/shard_map/pmax | solution.py:40
  292.2 0.5 exponential_reduce_fusion.1
  292.7 0.0 copy-done.3
  292.7 18.0 %psum.23 = f32[2048]{0:T(1024)S(1)} all-reduce(f32[2048]{0:T(1024)S(1)} %exponential_reduce_fusion.1), channel_id=1, replica_groups=mesh['noise'=8,'dp'=4] {'noise'}, use_global_device_ids=true, to_apply=%region_25.26 | all-reduce | flops 2048 | bytes 16384 | tf_op jit(solution)/shard_map/psum | solution.py:41
  310.7 0.0 copy-start.2
  310.7 0.3 fusion.8
  311.0 0.5 exponential_reduce_fusion
  311.6 5.1 %all-gather.15 = f32[4,1,256]{2,1,0:T(1,128)S(1)} all-gather(f32[1,1,256]{2,1,0:T(1,128)S(1)} %bitcast.98), channel_id=9, replica_groups=mesh['noise'=8,'dp'=4] {'dp'}, dimensions={0}, use_global_device_ids=true | all-gather | bytes 5120 | tf_op jit(solution)/shard_map/all_gather | solution.py:13
  316.6 5.1 %all-gather.14 = f32[4,1,256]{2,1,0:T(1,128)S(1)} all-gather(f32[1,1,256]{2,1,0:T(1,128)S(1)} %bitcast.91), channel_id=8, replica_groups=mesh['noise'=8,'dp'=4] {'dp'}, dimensions={0}, use_global_device_ids=true | all-gather | bytes 5120 | tf_op jit(solution)/shard_map/all_gather | solution.py:13
  321.7 0.1 while.71
  321.8 0.0 copy-done.2
  321.9 7.2 %fusion.9 = f32[256,2048]{1,0:T(8,128)} fusion(bf16[2048,2048]{1,0:T(8,128)(2,1)} %all-gather.21.cloned.1.call-done, f32[256,2048]{1,0:T(8,128)S(1)} %get-tuple-element.600, f32[256]{0:T(256)S(1)} %get-tuple-element.542, f32[256]{0:T(256)S(1)} %get-tuple-element.541, f32[2048]{0:T(1024)S(1)} %multiply_subtract_fusion), kind=kOutput, calls=%fused_computation.39 | convolution fusion | flops 2150105088 | bytes 12593152 | tf_op jit(solution)/shard_map/dot_general | solution.py:67
  329.0 0.0 reduce-scatter.2.cloned.1.call-update
  329.1 29.7 %reduce-scatter.2.cloned.1.call-done = f32[256,512]{1,0:T(8,128)} async-done(((f32[256,2048]{1,0:T(8,128)}), f32[256,512]{1,0:T(8,128)}) %reduce-scatter.2.cloned.1.call-update) | async-done | bytes 524304 | tf_op jit(solution)/shard_map/reduce_scatter | solution.py:68
  358.7 1.8 convert_element_type.15
  (46 shorter events, 0.4 us)
Async XLA Ops:
  7.2 21.8 %all-gather.19.cloned.1.call-start = ((), (), s32[]{:S(2)}) async-start(), calls=%async_computation.1 | async-start | bytes 1310720 | tf_op jit(solution)/shard_map/all_gather | solution.py:46
  7.9 148.2 %all-gather.21.cloned.1.call-start = ((), (), s32[]{:S(2)}) async-start(), calls=%async_computation.2 | async-start | bytes 9437184 | tf_op jit(solution)/shard_map/all_gather | solution.py:50
  8.6 350.1 %reduce-scatter.2.cloned.1.call-start = ((), (), s32[]{:S(2)}) async-start(), calls=%async_computation.3 | async-start | bytes 2621440 | tf_op jit(solution)/shard_map/reduce_scatter | solution.py:68
  29.0 132.3 %copy-start.1 = (bf16[256,2048]{1,0:T(8,128)(2,1)S(1)}, bf16[256,2048]{1,0:T(8,128)(2,1)}, u32[]{:S(2)}) copy-start(bf16[256,2048]{1,0:T(8,128)(2,1)} %all-gather.19.cloned.1.call-done) | copy-start | bytes 3145732
  156.1 5.8 %copy-start = (bf16[2048,2048]{1,0:T(8,128)(2,1)S(1)}, bf16[2048,2048]{1,0:T(8,128)(2,1)}, u32[]{:S(2)}) copy-start(bf16[2048,2048]{1,0:T(8,128)(2,1)} %all-gather.21.cloned.1.call-done) | copy-start | bytes 25165828
  273.1 19.5 %copy-start.3 = (f32[256]{0:T(256)}, f32[256]{0:T(256)S(1)}, u32[]{:S(2)}) copy-start(f32[256]{0:T(256)S(1)} %multiply_subtract_fusion.3) | copy-start | bytes 3076
  310.7 11.1 %copy-start.2 = (f32[2048]{0:T(1024)}, f32[2048]{0:T(1024)S(1)}, u32[]{:S(2)}) copy-start(f32[2048]{0:T(1024)S(1)} %multiply_subtract_fusion) | copy-start | bytes 24580
Sparse Core Ops, SparseCore 0:
  9.6 19.4 all-gather.18
  31.1 124.9 all-gather.20
  329.2 29.5 reduce-scatter.1
where the time goes:
time: 367 us
  waiting for transfers between devices  177 us (48%)
  blocking collectives  151 us (41%)
  other arithmetic  14.2 us (4%)
  between operations  14 us (4%)
  matrix products  10.1 us (3%)
    all_gather x1, waiting for transfers between devices, local(): block = lax.all_gather(data_latents, 'noise', axis=0, tiled=True)  126 us
    pmax x3, blocking collectives, column_lse(): top = lax.pmax(local_top, 'noise')  56.1 us
    psum x3, blocking collectives, column_lse(): total = lax.psum(jnp.sum(jnp.exp(scores - top[None, :]), axis=0), 'noise')  54.2 us
    all_gather x8, blocking collectives, merged(): gathered = jax.tree.map(lambda a: lax.all_gather(a, axis), part)  40.5 us
    reduce_scatter x1, waiting for transfers between devices, local(): lax.psum_scatter(partial_sum, 'dp', scatter_dimension=1, tiled=True)  29.7 us
    all_gather x1, waiting for transfers between devices, local(): rows = lax.all_gather(noise_latents, 'dp', axis=0, tiled=True)  20.3 us
  transfers between devices with their start and end apart: 3, of which 3 were waited for; matrix products, arithmetic and copies ran while one was open for 0% of the time, Pallas kernels for 0%

commit v1 on v0

v1 whole, which is shorter than its diff:
```python
import functools
import math

import jax
import jax.numpy as jnp
from jax import lax
from jax.experimental import pallas as pl
from jax.experimental.pallas import tpu as pltpu
from jax.sharding import PartitionSpec as P

ITERS = 3


smoothing = 0.05
LOG2E = math.log2(math.e)
MESH = pl.DeviceIdType.MESH
VMEM_LIMIT = 56 * 1024 * 1024


def exp2(a):
    return jnp.exp2(a)


def kernel(
    sizes, noise_ref, data_ref, out_ref, np_ref, dpot_ref,
    nz, dat, scores, w, vcol, lcol, ubuf, lbuf, ybuf, blane, fbuf,
    pk, csend, cbuf, xsend, xbuf, zsend, zbuf,
    dsem, zsem, xsem, csem, lsem, ysem, fsem, rcsem, rxsem, rzsem,
):
    Z, total_rows, total_cols = sizes
    piece, D = noise_ref.shape
    dpiece = data_ref.shape[0]
    rows = 4 * piece
    cols = 2 * dpiece
    width = D // 4
    n = lax.axis_index("noise")
    d = lax.axis_index("dp")
    z, y = n // 2, n % 2
    x, c = d // 2, d % 2
    id_y = (z * 2 + (1 - y), d)
    id_x = (n, (1 - x) * 2 + c)
    id_c = (n, x * 2 + (1 - c))

    def remote(src, dst, sems, index, device):
        return pltpu.make_async_remote_copy(
            src_ref=src, dst_ref=dst, send_sem=sems.at[(0,) + index], recv_sem=sems.at[(1,) + index],
            device_id=device, device_id_type=MESH,
        )

    group = [(zo, do) for zo in range(Z) for do in range(4) if (zo, do) != (0, 0)]

    def member(zo, do):
        return (((z + zo) % Z) * 2 + y, (d + do) % 4)

    barrier = pltpu.get_barrier_semaphore()
    for zo, do in group:
        pl.semaphore_signal(barrier, inc=1, device_id=member(zo, do), device_id_type=MESH)
    pl.semaphore_signal(barrier, inc=1, device_id=id_y, device_id_type=MESH)
    pl.semaphore_wait(barrier, len(group) + 1)

    to_y = remote(data_ref, dat.at[y], dsem, (0,), id_y)
    to_y.start()
    dat[y] = data_ref[...]

    def passed(k, up):
        p = z - k if up else z + k
        return p, (p >= 0 if up else p < Z)

    def along_z(k, up):
        p = z - k if up else z + k
        src = noise_ref if k == 0 else nz.at[p, d]
        return remote(src, nz.at[p, d], zsem, (int(up), k), ((z + 1 if up else z - 1) * 2 + y, d))

    def arrived_z(k, up):
        p = z - k if up else z + k
        return remote(nz.at[p, d], nz.at[p, d], zsem, (int(up), k - 1), ((z - 1 if up else z + 1) * 2 + y, d))

    def over_x(k, up):
        p = z - k if up else z + k
        src = noise_ref if k == 0 else nz.at[p, d]
        return remote(src, nz.at[p, d], xsem, (int(up), k), id_x)

    def arrived_x(k, up):
        p = z - k if up else z + k
        other = (1 - x) * 2 + c
        return remote(nz.at[p, other], nz.at[p, other], xsem, (int(up), k), id_x)

    def over_c(k, up, far):
        p = z - k if up else z + k
        mine = (1 - x) * 2 + c if far else d
        src = noise_ref if (k == 0 and not far) else nz.at[p, mine]
        return remote(src, nz.at[p, mine], csem, (int(far), int(up), k), id_c)

    def arrived_c(k, up, far):
        p = z - k if up else z + k
        theirs = (1 - x) * 2 + (1 - c) if far else x * 2 + (1 - c)
        return remote(nz.at[p, theirs], nz.at[p, theirs], csem, (int(far), int(up), k), id_c)

    def can_go(up):
        return z + 1 < Z if up else z >= 1

    def step_z(k):
        for up in (True, False):
            if k == 0:
                @pl.when(can_go(up))
                def _():
                    along_z(0, up).start()
                if up:
                    over_x(0, True).start()
                    over_c(0, True, False).start()
            else:
                @pl.when(passed(k, up)[1])
                def _():
                    arrived_z(k, up).wait_recv()

                    @pl.when(can_go(up))
                    def _():
                        along_z(k, up).start()
                    over_x(k, up).start()
                    over_c(k, up, False).start()

    def step_x(k):
        for up in (True, False):
            if k == 0 and not up:
                continue

            @pl.when(passed(k, up)[1])
            def _():
                arrived_x(k, up).wait_recv()
                over_c(k, up, True).start()

    step_z(0)
    nz[z, d] = noise_ref[...]
    for k in range(1, Z):
        step_z(k)
        step_x(k - 1)
    step_x(Z - 1)
    for k in range(Z):
        for up in (True, False):
            if k == 0 and not up:
                continue

            @pl.when(passed(k, up)[1])
            def _():
                arrived_c(k, up, False).wait_recv()
                arrived_c(k, up, True).wait_recv()
    remote(dat.at[1 - y], dat.at[1 - y], dsem, (0,), id_y).wait_recv()

    scale = 2.0 * LOG2E / (D * smoothing)
    norm_scale = LOG2E / (D * smoothing)

    def product(b, _):
        block = nz[b].reshape(rows, D)
        scores[:, pl.ds(pl.multiple_of(b * rows, rows), rows)] = scale * lax.dot_general(
            dat[...].reshape(cols, D), block, (((1,), (1,)), ((), ())), preferred_element_type=jnp.float32
        )
        return 0

    lax.fori_loop(0, Z, product, 0)

    def lane_sums(values):
        total = None
        for start in range(0, D, 128):
            part = values[:, start : start + 128].astype(jnp.float32)
            part = part * part
            total = part if total is None else total + part
        return total

    half = lcol
    for yy in range(2):
        half[yy * dpiece : (yy + 1) * dpiece, :] = lane_sums(dat.at[yy])
    blane[...] = jnp.sum(jnp.transpose(half[...]), axis=0, keepdims=True)
    vcol[...] = jnp.broadcast_to(
        -norm_scale * jnp.sum(half[...], axis=1, keepdims=True), (cols, 128)
    )

    def row_lse(r):
        me = z * 4 + d
        for start in range(0, Z * rows, 128):
            t = scores[:, start : start + 128] + vcol[...]
            top = jnp.max(t, axis=0, keepdims=True)
            total = jnp.sum(exp2(t - top), axis=0, keepdims=True)
            lbuf[r, me, :, start : start + 128] = top + jnp.log2(total)
        for zo, do in group:
            remote(lbuf.at[r, me], lbuf.at[r, me], lsem, (r, zo, do), member(zo, do)).start()
        for zo, do in group:
            src = ((z + Z - zo) % Z) * 4 + (d + 4 - do) % 4
            remote(lbuf.at[r, src], lbuf.at[r, src], lsem, (r, zo, do), member(zo, do)).wait_recv()
        parts = [lbuf[r, s] for s in range(4 * Z)]
        top = functools.reduce(jnp.maximum, parts)
        total = functools.reduce(jnp.add, [exp2(a - top) for a in parts])
        return top + jnp.log2(total)

    def pair_lse(a, b):
        top = jnp.maximum(a, b)
        return top + jnp.log2(exp2(a - top) + exp2(b - top))

    def column_lse(r):
        chunk = 64 if cols % 64 == 0 else cols
        for start in range(0, cols, chunk):
            t = scores[start : start + chunk, :] + ubuf[...]
            top = jnp.max(t, axis=1, keepdims=True)
            total = jnp.sum(exp2(t - top), axis=1, keepdims=True)
            lcol[start : start + chunk, :] = jnp.broadcast_to(top, (chunk, 128)) + jnp.log2(
                jnp.broadcast_to(total, (chunk, 128))
            )
        ybuf[r, y] = jnp.transpose(lcol[...])[0:1, :]
        remote(ybuf.at[r, y], ybuf.at[r, y], ysem, (r,), id_y).start()
        remote(ybuf.at[r, 1 - y], ybuf.at[r, 1 - y], ysem, (r,), id_y).wait_recv()
        lane = pair_lse(ybuf[r, 0], ybuf[r, 1])
        vcol[...] = jnp.transpose(jnp.broadcast_to(-math.log2(total_cols) - lane, (128, cols)))
        return lane

    for it in range(ITERS):
        lse = row_lse(it)
        ubuf[...] = -math.log2(total_rows) - lse
        lane = column_lse(it)

    fbuf[z] = -smoothing * math.log(total_cols) - (smoothing / LOG2E) * lane + blane[...] / D
    for zo in range(1, Z):
        remote(fbuf.at[z], fbuf.at[z], fsem, (zo,), member(zo, 0)).start()
    own_norms = jnp.sum(jnp.transpose(lane_sums(nz[z].reshape(rows, D))), axis=0, keepdims=True)
    own_u = ubuf[:, pl.ds(pl.multiple_of(z * rows, rows), rows)]
    np_ref[...] = (
        -smoothing * math.log(total_rows)
        + (smoothing / LOG2E) * (own_u + math.log2(total_rows))
        + own_norms / D
    )

    ubuf[...] = row_lse(ITERS)
    for b in range(Z):
        for start in range(0, rows, 128):
            at = b * rows + start
            t = scores[:, at : at + 128] + vcol[...] - ubuf[:, at : at + 128]
            w[b, start : start + 128, :] = jnp.transpose(exp2(t)).astype(jnp.bfloat16)

    def block(b, column):
        return jnp.dot(
            w[b],
            dat[:, :, pl.ds(pl.multiple_of(column * width, width), width)].reshape(cols, width),
            preferred_element_type=jnp.float32,
        )

    def core_copy(off, far):
        return remote(csend.at[off, far], cbuf.at[off, far], rcsem, (off, far), id_c)

    def x_copy(off):
        return remote(xsend.at[off], xbuf.at[off], rxsem, (off,), id_x)

    def z_copy(off):
        return remote(zsend.at[off - 1], zbuf.at[off - 1], rzsem, (off,), member(off, 0))

    def products(off):
        b = (z + off) % Z
        for far in (1, 0):
            side = 1 - x if far else x
            csend[off, far] = block(b, side * 2 + (1 - c))
            core_copy(off, far).start()
            pk[off, far] = block(b, side * 2 + c)

    def send_x(off):
        core_copy(off, 1).wait_recv()
        xsend[off] = (pk[off, 1] + cbuf[off, 1]).astype(jnp.bfloat16)
        x_copy(off).start()

    order = [Z // 2] + [o for o in range(1, Z) if o != Z // 2] + [0]
    for place, off in enumerate(order):
        products(off)
        if place >= 1:
            send_x(order[place - 1])
    send_x(order[-1])
    for off in order:
        core_copy(off, 0).wait_recv()
        x_copy(off).wait_recv()
        total = pk[off, 0] + cbuf[off, 0] + xbuf[off].astype(jnp.float32)
        if off:
            zsend[off - 1] = total.astype(jnp.bfloat16)
            z_copy(off).start()
        else:
            pk[0, 0] = total
    for zo in range(1, Z):
        src = (z + Z - zo) % Z
        remote(fbuf.at[src], fbuf.at[src], fsem, (zo,), member(zo, 0)).wait_recv()
    dpot_ref[...] = fbuf[...]
    total = pk[0, 0]
    for off in range(1, Z):
        z_copy(off).wait_recv()
        total = total + zbuf[off - 1].astype(jnp.float32)
    out_ref[...] = total.astype(jnp.bfloat16)

    to_y.wait_send()
    for k in range(Z):
        for up in (True, False):
            if k == Z - 1:
                pass
            else:
                @pl.when(jnp.logical_and(passed(k, up)[1], can_go(up)))
                def _():
                    along_z(k, up).wait_send()
            if k == 0 and not up:
                continue

            @pl.when(passed(k, up)[1])
            def _():
                over_x(k, up).wait_send()
                over_c(k, up, False).wait_send()
                over_c(k, up, True).wait_send()
    me = z * 4 + d
    for r in range(ITERS + 1):
        for zo, do in group:
            remote(lbuf.at[r, me], lbuf.at[r, me], lsem, (r, zo, do), member(zo, do)).wait_send()
    for r in range(ITERS):
        remote(ybuf.at[r, y], ybuf.at[r, y], ysem, (r,), id_y).wait_send()
    for zo in range(1, Z):
        remote(fbuf.at[z], fbuf.at[z], fsem, (zo,), member(zo, 0)).wait_send()
    for off in range(Z):
        core_copy(off, 0).wait_send()
        core_copy(off, 1).wait_send()
        x_copy(off).wait_send()
        if off:
            z_copy(off).wait_send()


def scratch(Z, piece, dpiece, D):
    rows, cols, width = 4 * piece, 2 * dpiece, D // 4
    bf16, f32 = jnp.bfloat16, jnp.float32
    arrays = [
        ((Z, 4, piece, D), bf16),
        ((2, dpiece, D), bf16),
        ((cols, Z * rows), f32),
        ((Z, rows, cols), bf16),
        ((cols, 128), f32),
        ((cols, 128), f32),
        ((1, Z * rows), f32),
        ((ITERS + 1, 4 * Z, 1, Z * rows), f32),
        ((ITERS, 2, 1, cols), f32),
        ((1, cols), f32),
        ((Z, 1, cols), f32),
        ((Z, 2, rows, width), f32),
        ((Z, 2, rows, width), f32),
        ((Z, 2, rows, width), f32),
        ((Z, rows, width), bf16),
        ((Z, rows, width), bf16),
        ((Z - 1, rows, width), bf16),
        ((Z - 1, rows, width), bf16),
    ]
    sems = [
        (2, 1), (2, 2, Z), (2, 2, Z), (2, 2, 2, Z), (2, ITERS + 1, Z, 4), (2, ITERS), (2, Z),
        (2, Z, 2), (2, Z), (2, Z),
    ]
    return arrays, sems


def tiled_local(Z, total_rows, total_cols, noise_latents, data_latents):
    piece, D = noise_latents.shape
    dpiece = data_latents.shape[0]
    rows, cols, width = 4 * piece, 2 * dpiece, D // 4
    arrays, sems = scratch(Z, piece, dpiece, D)
    vmem = pl.BlockSpec(memory_space=pltpu.VMEM)
    paired, noise_potential, data_potential = pl.pallas_call(
        functools.partial(kernel, (Z, total_rows, total_cols)),
        out_shape=(
            jax.ShapeDtypeStruct((rows, width), jnp.bfloat16),
            jax.ShapeDtypeStruct((1, rows), jnp.float32),
            jax.ShapeDtypeStruct((Z, 1, cols), jnp.float32),
        ),
        in_specs=[vmem, vmem],
        out_specs=(vmem, vmem, vmem),
        scratch_shapes=[pltpu.VMEM(s, t) for s, t in arrays] + [pltpu.SemaphoreType.DMA(s) for s in sems],
        compiler_params=pltpu.CompilerParams(
            collective_id=0, has_side_effects=True, vmem_limit_bytes=VMEM_LIMIT
        ),
    )(noise_latents, data_latents)
    return paired, noise_potential.reshape(rows), data_potential.reshape(Z * cols)


def gathered_lse(scores, axis, name):
    top = lax.pmax(jnp.max(scores, axis=axis), name)
    total = lax.psum(jnp.sum(jnp.exp(scores - jnp.expand_dims(top, axis)), axis=axis), name)
    return top + jnp.log(total)


def gathered_local(total_rows, total_cols, noise_latents, data_latents):
    rows = lax.all_gather(noise_latents, "dp", axis=0, tiled=True)
    block = lax.all_gather(data_latents, "noise", axis=0, tiled=True)
    row_norms = jnp.sum(jnp.square(rows.astype(jnp.float32)), axis=1)
    col_norms = jnp.sum(jnp.square(block.astype(jnp.float32)), axis=1)
    inner = jnp.dot(rows, block.T, preferred_element_type=jnp.float32)
    cost = (row_norms[:, None] + col_norms[None, :] - 2.0 * inner) / rows.shape[1]
    data_potential = jnp.zeros((cost.shape[1],), jnp.float32)
    for _ in range(ITERS):
        lse = gathered_lse((data_potential[None, :] - cost) / smoothing, 1, "dp")
        noise_potential = -smoothing * math.log(total_rows) - smoothing * lse
        lse = gathered_lse((noise_potential[:, None] - cost) / smoothing, 0, "noise")
        data_potential = -smoothing * math.log(total_cols) - smoothing * lse
    scores = (data_potential[None, :] - cost) / smoothing
    lse = gathered_lse(scores, 1, "dp")
    weights = jnp.exp(scores - lse[:, None]).astype(jnp.bfloat16)
    partial_sum = jnp.dot(weights, block, preferred_element_type=jnp.float32)
    paired_target = lax.psum_scatter(partial_sum, "dp", scatter_dimension=1, tiled=True)
    return paired_target.astype(jnp.bfloat16), noise_potential, data_potential


def solution(mesh):
    noise_size, dp_size = mesh.shape["noise"], mesh.shape["dp"]

    def local(noise_latents, data_latents):
        piece, D = noise_latents.shape
        dpiece = data_latents.shape[0]
        devices = noise_size * dp_size
        totals = (piece * devices, dpiece * devices)
        Z = noise_size // 2
        fits = noise_size % 2 == 0 and dp_size == 4 and Z >= 2
        if fits:
            arrays = scratch(Z, piece, dpiece, D)[0]
            fits = sum(math.prod(s) * jnp.dtype(t).itemsize for s, t in arrays) < VMEM_LIMIT * 3 // 4
        if fits:
            return tiled_local(Z, *totals, noise_latents, data_latents)
        return gathered_local(*totals, noise_latents, data_latents)

    return jax.shard_map(
        local,
        mesh=mesh,
        in_specs=(P(("noise", "dp"), None), P(("dp", "noise"), None)),
        out_specs=(P("noise", "dp"), P("noise"), P("dp")),
        check_vma=False,
    )
```

time: 367 us -> 109 us (0.30)
  waiting for transfers between devices: 177 us -> 0 us
  blocking collectives: 151 us -> 0 us
  Pallas kernels: 0 us -> 105 us
  other arithmetic: 14.2 us -> 0 us
  between operations: 14 us -> 0.66 us
  matrix products: 10.1 us -> 0 us
    all_gather x2 -> x0, waiting for transfers between devices: 146 us -> none  [the longest x1 126 us: local(): block = lax.all_gather(data_latents, 'noise', axis=0, tiled=True)]
    pallas_call x0 -> x1, Pallas kernels: none -> 105 us  [tiled_local(): pl.pallas_call(functools.partial(kernel, (Z, total_rows, total_cols)), ou...]
    pmax x3 -> x0, blocking collectives: 56.1 us -> none  [column_lse(): top = lax.pmax(local_top, 'noise')]
    psum x3 -> x0, blocking collectives: 54.2 us -> none  [column_lse(): total = lax.psum(jnp.sum(jnp.exp(scores - top[None, :]), axis=0), 'noise')]
    all_gather x8 -> x0, blocking collectives: 40.5 us -> none  [merged(): gathered = jax.tree.map(lambda a: lax.all_gather(a, axis), part)]
    reduce_scatter x1 -> x0, waiting for transfers between devices: 29.7 us -> none  [local(): lax.psum_scatter(partial_sum, 'dp', scatter_dimension=1, tiled=True)]
    reduce_sum x9 -> x0, other arithmetic: 10.4 us -> none  [the longest x1 5.23 us: local(): piece_norms = jnp.sum(jnp.square(block.astype(jnp.float32)), axis=1)]
    dot_general x2 -> x0, matrix products: 10.1 us -> none  [the longest x1 7.19 us: local(): partial_sum = jnp.dot(weights, block, preferred_element_type=jnp.float32)]
  transfers between devices with their start and end apart: 3 -> 0, of which waited for: 3 -> 0; matrix products, arithmetic and copies ran while one was open for 0% -> 0% of each run, Pallas kernels for 0% -> 0%
where the time goes in v1:
time: 109 us
  Pallas kernels  105 us (96%)
  local copies, waits for them, and re-layouts  2.85 us (3%)
    pallas_call x1, Pallas kernels, tiled_local(): pl.pallas_call(functools.partial(kernel, (Z, total_rows, total_cols)), ou...  105 us
    unnamed x7, local copies, waits for them, and re-layouts  2.85 us

profile of v1, /device:TPU:0, one launch (start us, length us, event | category | flops | bytes accessed | tf_op | source)
XLA Modules:
  0.0 108.8 jit_solution(6000509169433996600)
XLA Ops:
  0.6 105.3 %shard_map.49 = (bf16[256,512]{1,0:T(8,128)(2,1)}, f32[1,256]{1,0:T(1,128)}, f32[4,1,512]{2,1,0:T(1,128)}) custom-call(bf16[64,2048]{1,0:T(8,128)(2,1)} %noise_ref.1, bf16[256,2048]{1,0:T(8,128)(2,1)} %data_ref.1), custom_call_target="tpu_custom_call" | custom-call | tf_op jit(solution)/shard_map/pallas_call | solution.py:360
  105.9 0.0 copy-start.1
  106.0 0.0 copy-start
  106.0 1.7 %copy.8 = bf16[256,512]{1,0:T(8,128)(2,1)} copy(bf16[256,512]{1,0:T(8,128)(2,1)} %get-tuple-element.12) | data formatting | bytes 524288
  107.6 0.0 copy-done.1
  107.6 0.6 copy.9
  108.2 0.0 copy-done
  108.2 0.6 copy.10
Async XLA Ops:
  105.9 1.7 %copy-start.1 = (f32[1,256]{1,0:T(1,128)S(1)}, f32[1,256]{1,0:T(1,128)}, u32[]{:S(2)}) copy-start(f32[1,256]{1,0:T(1,128)} %get-tuple-element.7) | copy-start | bytes 3076
  106.0 2.3 %copy-start = (f32[4,1,512]{2,1,0:T(1,128)S(1)}, f32[4,1,512]{2,1,0:T(1,128)}, u32[]{:S(2)}) copy-start(f32[4,1,512]{2,1,0:T(1,128)} %get-tuple-element.8) | copy-start | bytes 24580

commit v2 on v1

--- a/solution.py
+++ b/solution.py
@@ -25,7 +25,7 @@
     sizes, noise_ref, data_ref, out_ref, np_ref, dpot_ref,
     nz, dat, scores, w, vcol, lcol, ubuf, lbuf, ybuf, blane, fbuf,
     pk, csend, cbuf, xsend, xbuf, zsend, zbuf,
-    dsem, zsem, xsem, csem, lsem, ysem, fsem, rcsem, rxsem, rzsem,
+    sent, dsem, zout, zsem, xsem, csem, lsem, ysem, fsem, rcsem, rxsem, rzsem,
 ):
     Z, total_rows, total_cols = sizes
     piece, D = noise_ref.shape
@@ -41,11 +41,13 @@
     id_x = (n, (1 - x) * 2 + c)
     id_c = (n, x * 2 + (1 - c))
 
-    def remote(src, dst, sems, index, device):
+    def remote(src, dst, send_sem, recv_sem, device):
         return pltpu.make_async_remote_copy(
-            src_ref=src, dst_ref=dst, send_sem=sems.at[(0,) + index], recv_sem=sems.at[(1,) + index],
+            src_ref=src, dst_ref=dst, send_sem=send_sem, recv_sem=recv_sem,
             device_id=device, device_id_type=MESH,
         )
+
+    X, C, L, Y, F, RC, RX, RZ, DATA = range(9)
 
     group = [(zo, do) for zo in range(Z) for do in range(4) if (zo, do) != (0, 0)]
 
@@ -58,7 +60,7 @@
     pl.semaphore_signal(barrier, inc=1, device_id=id_y, device_id_type=MESH)
     pl.semaphore_wait(barrier, len(group) + 1)
 
-    to_y = remote(data_ref, dat.at[y], dsem, (0,), id_y)
+    to_y = remote(data_ref, dat.at[y], sent.at[DATA], dsem.at[0], id_y)
     to_y.start()
     dat[y] = data_ref[...]
 
@@ -69,32 +71,27 @@
     def along_z(k, up):
         p = z - k if up else z + k
         src = noise_ref if k == 0 else nz.at[p, d]
-        return remote(src, nz.at[p, d], zsem, (int(up), k), ((z + 1 if up else z - 1) * 2 + y, d))
+        return remote(src, nz.at[p, d], zout.at[int(up), k], zsem.at[int(up), k], ((z + 1 if up else z - 1) * 2 + y, d))
 
     def arrived_z(k, up):
         p = z - k if up else z + k
-        return remote(nz.at[p, d], nz.at[p, d], zsem, (int(up), k - 1), ((z - 1 if up else z + 1) * 2 + y, d))
+        return remote(nz.at[p, d], nz.at[p, d], zout.at[int(up), k], zsem.at[int(up), k - 1], ((z - 1 if up else z + 1) * 2 + y, d))
 
     def over_x(k, up):
         p = z - k if up else z + k
         src = noise_ref if k == 0 else nz.at[p, d]
-        return remote(src, nz.at[p, d], xsem, (int(up), k), id_x)
+        return remote(src, nz.at[p, d], sent.at[X], xsem.at[int(up), k], id_x)
 
     def arrived_x(k, up):
         p = z - k if up else z + k
         other = (1 - x) * 2 + c
-        return remote(nz.at[p, other], nz.at[p, other], xsem, (int(up), k), id_x)
+        return remote(nz.at[p, other], nz.at[p, other], sent.at[X], xsem.at[int(up), k], id_x)
 
     def over_c(k, up, far):
         p = z - k if up else z + k
         mine = (1 - x) * 2 + c if far else d
         src = noise_ref if (k == 0 and not far) else nz.at[p, mine]
-        return remote(src, nz.at[p, mine], csem, (int(far), int(up), k), id_c)
-
-    def arrived_c(k, up, far):
-        p = z - k if up else z + k
-        theirs = (1 - x) * 2 + (1 - c) if far else x * 2 + (1 - c)
-        return remote(nz.at[p, theirs], nz.at[p, theirs], csem, (int(far), int(up), k), id_c)
+        return remote(src, nz.at[p, mine], sent.at[C], csem.at[0], id_c)
 
     def can_go(up):
         return z + 1 < Z if up else z >= 1
@@ -135,29 +132,6 @@
         step_z(k)
         step_x(k - 1)
     step_x(Z - 1)
-    for k in range(Z):
-        for up in (True, False):
-            if k == 0 and not up:
-                continue
-
-            @pl.when(passed(k, up)[1])
-            def _():
-                arrived_c(k, up, False).wait_recv()
-                arrived_c(k, up, True).wait_recv()
-    remote(dat.at[1 - y], dat.at[1 - y], dsem, (0,), id_y).wait_recv()
-
-    scale = 2.0 * LOG2E / (D * smoothing)
-    norm_scale = LOG2E / (D * smoothing)
-
-    def product(b, _):
-        block = nz[b].reshape(rows, D)
-        scores[:, pl.ds(pl.multiple_of(b * rows, rows), rows)] = scale * lax.dot_general(
-            dat[...].reshape(cols, D), block, (((1,), (1,)), ((), ())), preferred_element_type=jnp.float32
-        )
-        return 0
-
-    lax.fori_loop(0, Z, product, 0)
-
     def lane_sums(values):
         total = None
         for start in range(0, D, 128):
@@ -166,12 +140,28 @@
             total = part if total is None else total + part
         return total
 
-    half = lcol
-    for yy in range(2):
-        half[yy * dpiece : (yy + 1) * dpiece, :] = lane_sums(dat.at[yy])
-    blane[...] = jnp.sum(jnp.transpose(half[...]), axis=0, keepdims=True)
+    lcol[pl.ds(pl.multiple_of(y * dpiece, dpiece), dpiece), :] = lane_sums(data_ref)
+
+    half_noise = nz.at[:, 0:2]
+    remote(half_noise, half_noise, sent.at[C], csem.at[0], id_c).wait_recv()
+    remote(dat.at[1 - y], dat.at[1 - y], sent.at[DATA], dsem.at[0], id_y).wait_recv()
+    lcol[pl.ds(pl.multiple_of((1 - y) * dpiece, dpiece), dpiece), :] = lane_sums(dat.at[1 - y])
+
+    scale = 2.0 * LOG2E / (D * smoothing)
+    norm_scale = LOG2E / (D * smoothing)
+
+    def product(b, _):
+        block = nz[b].reshape(rows, D)
+        scores[:, pl.ds(pl.multiple_of(b * rows, rows), rows)] = scale * lax.dot_general(
+            dat[...].reshape(cols, D), block, (((1,), (1,)), ((), ())), preferred_element_type=jnp.float32
+        )
+        return 0
+
+    lax.fori_loop(0, Z, product, 0)
+
+    blane[...] = jnp.sum(jnp.transpose(lcol[...]), axis=0, keepdims=True)
     vcol[...] = jnp.broadcast_to(
-        -norm_scale * jnp.sum(half[...], axis=1, keepdims=True), (cols, 128)
+        -norm_scale * jnp.sum(lcol[...], axis=1, keepdims=True), (cols, 128)
     )
 
     def row_lse(r):
@@ -182,10 +172,9 @@
             total = jnp.sum(exp2(t - top), axis=0, keepdims=True)
             lbuf[r, me, :, start : start + 128] = top + jnp.log2(total)
         for zo, do in group:
-            remote(lbuf.at[r, me], lbuf.at[r, me], lsem, (r, zo, do), member(zo, do)).start()
-        for zo, do in group:
-            src = ((z + Z - zo) % Z) * 4 + (d + 4 - do) % 4
-            remote(lbuf.at[r, src], lbuf.at[r, src], lsem, (r, zo, do), member(zo, do)).wait_recv()
+            remote(lbuf.at[r, me], lbuf.at[r, me], sent.at[L], lsem.at[r], member(zo, do)).start()
+        others = lbuf.at[r, 0 : 4 * Z - 1]
+        remote(others, others, sent.at[L], lsem.at[r], id_c).wait_recv()
         parts = [lbuf[r, s] for s in range(4 * Z)]
         top = functools.reduce(jnp.maximum, parts)
         total = functools.reduce(jnp.add, [exp2(a - top) for a in parts])
@@ -205,8 +194,8 @@
                 jnp.broadcast_to(total, (chunk, 128))
             )
         ybuf[r, y] = jnp.transpose(lcol[...])[0:1, :]
-        remote(ybuf.at[r, y], ybuf.at[r, y], ysem, (r,), id_y).start()
-        remote(ybuf.at[r, 1 - y], ybuf.at[r, 1 - y], ysem, (r,), id_y).wait_recv()
+        remote(ybuf.at[r, y], ybuf.at[r, y], sent.at[Y], ysem.at[r], id_y).start()
+        remote(ybuf.at[r, 1 - y], ybuf.at[r, 1 - y], sent.at[Y], ysem.at[r], id_y).wait_recv()
         lane = pair_lse(ybuf[r, 0], ybuf[r, 1])
         vcol[...] = jnp.transpose(jnp.broadcast_to(-math.log2(total_cols) - lane, (128, cols)))
         return lane
@@ -218,7 +207,7 @@
 
     fbuf[z] = -smoothing * math.log(total_cols) - (smoothing / LOG2E) * lane + blane[...] / D
     for zo in range(1, Z):
-        remote(fbuf.at[z], fbuf.at[z], fsem, (zo,), member(zo, 0)).start()
+        remote(fbuf.at[z], fbuf.at[z], sent.at[F], fsem.at[0], member(zo, 0)).start()
     own_norms = jnp.sum(jnp.transpose(lane_sums(nz[z].reshape(rows, D))), axis=0, keepdims=True)
     own_u = ubuf[:, pl.ds(pl.multiple_of(z * rows, rows), rows)]
     np_ref[...] = (
@@ -234,95 +223,89 @@
             t = scores[:, at : at + 128] + vcol[...] - ubuf[:, at : at + 128]
             w[b, start : start + 128, :] = jnp.transpose(exp2(t)).astype(jnp.bfloat16)
 
-    def block(b, column):
+    part = rows // 2
+
+    def block(b, h, column):
         return jnp.dot(
-            w[b],
+            w[b, h * part : (h + 1) * part, :],
             dat[:, :, pl.ds(pl.multiple_of(column * width, width), width)].reshape(cols, width),
             preferred_element_type=jnp.float32,
         )
 
-    def core_copy(off, far):
-        return remote(csend.at[off, far], cbuf.at[off, far], rcsem, (off, far), id_c)
-
-    def x_copy(off):
-        return remote(xsend.at[off], xbuf.at[off], rxsem, (off,), id_x)
-
-    def z_copy(off):
-        return remote(zsend.at[off - 1], zbuf.at[off - 1], rzsem, (off,), member(off, 0))
-
-    def products(off):
+    def core_copy(off, h, far):
+        return remote(
+            csend.at[off, far, h], cbuf.at[off, far, h], sent.at[RC], rcsem.at[off, far, h], id_c
+        )
+
+    def x_copy(off, h):
+        return remote(xsend.at[off, h], xbuf.at[off, h], sent.at[RX], rxsem.at[off, h], id_x)
+
+    def z_copy(off, h):
+        return remote(zsend.at[off - 1, h], zbuf.at[off - 1, h], sent.at[RZ], rzsem.at[0], member(off, 0))
+
+    def products(off, h):
         b = (z + off) % Z
         for far in (1, 0):
             side = 1 - x if far else x
-            csend[off, far] = block(b, side * 2 + (1 - c))
-            core_copy(off, far).start()
-            pk[off, far] = block(b, side * 2 + c)
-
-    def send_x(off):
-        core_copy(off, 1).wait_recv()
-        xsend[off] = (pk[off, 1] + cbuf[off, 1]).astype(jnp.bfloat16)
-        x_copy(off).start()
-
-    order = [Z // 2] + [o for o in range(1, Z) if o != Z // 2] + [0]
-    for place, off in enumerate(order):
-        products(off)
-        if place >= 1:
-            send_x(order[place - 1])
-    send_x(order[-1])
-    for off in order:
-        core_copy(off, 0).wait_recv()
-        x_copy(off).wait_recv()
-        total = pk[off, 0] + cbuf[off, 0] + xbuf[off].astype(jnp.float32)
+            csend[off, far, h] = block(b, h, side * 2 + (1 - c))
+            core_copy(off, h, far).start()
+            pk[off, far, h] = block(b, h, side * 2 + c)
+
+    def send_x(off, h):
+        core_copy(off, h, 1).wait_recv()
+        xsend[off, h] = (pk[off, 1, h] + cbuf[off, 1, h]).astype(jnp.bfloat16)
+        x_copy(off, h).start()
+
+    def finish(off, h):
+        core_copy(off, h, 0).wait_recv()
+        x_copy(off, h).wait_recv()
+        total = pk[off, 0, h] + cbuf[off, 0, h] + xbuf[off, h].astype(jnp.float32)
         if off:
-            zsend[off - 1] = total.astype(jnp.bfloat16)
-            z_copy(off).start()
+            zsend[off - 1, h] = total.astype(jnp.bfloat16)
+            z_copy(off, h).start()
         else:
-            pk[0, 0] = total
-    for zo in range(1, Z):
-        src = (z + Z - zo) % Z
-        remote(fbuf.at[src], fbuf.at[src], fsem, (zo,), member(zo, 0)).wait_recv()
+            pk[0, 0, h] = total
+
+    offsets = [Z // 2] + [o for o in range(1, Z) if o != Z // 2] + [0]
+    order = [(off, h) for off in offsets for h in range(2)]
+    for place in range(len(order) + 3):
+        if place < len(order):
+            products(*order[place])
+        if 1 <= place <= len(order):
+            send_x(*order[place - 1])
+        if place >= 3:
+            finish(*order[place - 3])
+    others = fbuf.at[0 : Z - 1]
+    remote(others, others, sent.at[F], fsem.at[0], id_c).wait_recv()
     dpot_ref[...] = fbuf[...]
-    total = pk[0, 0]
-    for off in range(1, Z):
-        z_copy(off).wait_recv()
-        total = total + zbuf[off - 1].astype(jnp.float32)
-    out_ref[...] = total.astype(jnp.bfloat16)
+    remote(zbuf, zbuf, sent.at[RZ], rzsem.at[0], id_c).wait_recv()
+    for h in range(2):
+        total = pk[0, 0, h]
+        for off in range(1, Z):
+            total = total + zbuf[off - 1, h].astype(jnp.float32)
+        out_ref[h * part : (h + 1) * part, :] = total.astype(jnp.bfloat16)
 
     to_y.wait_send()
-    for k in range(Z):
+    for k in range(Z - 1):
         for up in (True, False):
-            if k == Z - 1:
-                pass
-            else:
-                @pl.when(jnp.logical_and(passed(k, up)[1], can_go(up)))
-                def _():
-                    along_z(k, up).wait_send()
-            if k == 0 and not up:
-                continue
-
-            @pl.when(passed(k, up)[1])
+            @pl.when(jnp.logical_and(passed(k, up)[1], can_go(up)))
             def _():
-                over_x(k, up).wait_send()
-                over_c(k, up, False).wait_send()
-                over_c(k, up, True).wait_send()
-    me = z * 4 + d
-    for r in range(ITERS + 1):
-        for zo, do in group:
-            remote(lbuf.at[r, me], lbuf.at[r, me], lsem, (r, zo, do), member(zo, do)).wait_send()
-    for r in range(ITERS):
-        remote(ybuf.at[r, y], ybuf.at[r, y], ysem, (r,), id_y).wait_send()
-    for zo in range(1, Z):
-        remote(fbuf.at[z], fbuf.at[z], fsem, (zo,), member(zo, 0)).wait_send()
-    for off in range(Z):
-        core_copy(off, 0).wait_send()
-        core_copy(off, 1).wait_send()
-        x_copy(off).wait_send()
-        if off:
-            z_copy(off).wait_send()
+                along_z(k, up).wait_send()
+    remote(nz.at[:, 0], nz.at[:, 0], sent.at[X], xsem.at[0, 0], id_x).wait_send()
+    remote(half_noise, half_noise, sent.at[C], csem.at[0], id_c).wait_send()
+    others = lbuf.at[:, 0 : 4 * Z - 1]
+    remote(others, others, sent.at[L], lsem.at[0], id_c).wait_send()
+    remote(ybuf.at[:, 0], ybuf.at[:, 0], sent.at[Y], ysem.at[0], id_y).wait_send()
+    others = fbuf.at[0 : Z - 1]
+    remote(others, others, sent.at[F], fsem.at[0], id_c).wait_send()
+    remote(csend, cbuf, sent.at[RC], rcsem.at[0, 0, 0], id_c).wait_send()
+    remote(xsend, xbuf, sent.at[RX], rxsem.at[0, 0], id_x).wait_send()
+    remote(zsend, zbuf, sent.at[RZ], rzsem.at[0], id_c).wait_send()
 
 
 def scratch(Z, piece, dpiece, D):
     rows, cols, width = 4 * piece, 2 * dpiece, D // 4
+    part = rows // 2
     bf16, f32 = jnp.bfloat16, jnp.float32
     arrays = [
         ((Z, 4, piece, D), bf16),
@@ -336,18 +319,15 @@
         ((ITERS, 2, 1, cols), f32),
         ((1, cols), f32),
         ((Z, 1, cols), f32),
-        ((Z, 2, rows, width), f32),
-        ((Z, 2, rows, width), f32),
-        ((Z, 2, rows, width), f32),
-        ((Z, rows, width), bf16),
-        ((Z, rows, width), bf16),
-        ((Z - 1, rows, width), bf16),
-        ((Z - 1, rows, width), bf16),
+        ((Z, 2, 2, part, width), f32),
+        ((Z, 2, 2, part, width), f32),
+        ((Z, 2, 2, part, width), f32),
+        ((Z, 2, part, width), bf16),
+        ((Z, 2, part, width), bf16),
+        ((Z - 1, 2, part, width), bf16),
+        ((Z - 1, 2, part, width), bf16),
     ]
-    sems = [
-        (2, 1), (2, 2, Z), (2, 2, Z), (2, 2, 2, Z), (2, ITERS + 1, Z, 4), (2, ITERS), (2, Z),
-        (2, Z, 2), (2, Z), (2, Z),
-    ]
+    sems = [(9,), (1,), (2, Z), (2, Z), (2, Z), (1,), (ITERS + 1,), (ITERS,), (1,), (Z, 2, 2), (Z, 2), (1,)]
     return arrays, sems
 
 

time: 109 us -> 104 us (0.954)
  Pallas kernels: 105 us -> 100 us
    pallas_call x1, Pallas kernels: 105 us -> 100 us  [tiled_local(): pl.pallas_call(functools.partial(kernel, (Z, total_rows, total_cols)), ou...]
where the time goes in v2:
time: 104 us
  Pallas kernels  100 us (96%)
  local copies, waits for them, and re-layouts  2.85 us (3%)
    pallas_call x1, Pallas kernels, tiled_local(): pl.pallas_call(functools.partial(kernel, (Z, total_rows, total_cols)), ou...  100 us
    unnamed x7, local copies, waits for them, and re-layouts  2.85 us

profile of v2, /device:TPU:0, one launch (start us, length us, event | category | flops | bytes accessed | tf_op | source)
XLA Modules:
  0.0 103.7 jit_solution(9336122833183362274)
XLA Ops:
  0.6 100.2 %shard_map.49 = (bf16[256,512]{1,0:T(8,128)(2,1)}, f32[1,256]{1,0:T(1,128)}, f32[4,1,512]{2,1,0:T(1,128)}) custom-call(bf16[64,2048]{1,0:T(8,128)(2,1)} %noise_ref.1, bf16[256,2048]{1,0:T(8,128)(2,1)} %data_ref.1), custom_call_target="tpu_custom_call" | custom-call | tf_op jit(solution)/shard_map/pallas_call | solution.py:340
  100.9 0.0 copy-start.1
  100.9 0.0 copy-start
  100.9 1.7 %copy.8 = bf16[256,512]{1,0:T(8,128)(2,1)} copy(bf16[256,512]{1,0:T(8,128)(2,1)} %get-tuple-element.12) | data formatting | bytes 524288
  102.6 0.0 copy-done.1
  102.6 0.6 copy.9
  103.1 0.0 copy-done
  103.1 0.6 copy.10
Async XLA Ops:
  100.9 1.7 %copy-start.1 = (f32[1,256]{1,0:T(1,128)S(1)}, f32[1,256]{1,0:T(1,128)}, u32[]{:S(2)}) copy-start(f32[1,256]{1,0:T(1,128)} %get-tuple-element.7) | copy-start | bytes 3076
  100.9 2.3 %copy-start = (f32[4,1,512]{2,1,0:T(1,128)S(1)}, f32[4,1,512]{2,1,0:T(1,128)}, u32[]{:S(2)}) copy-start(f32[4,1,512]{2,1,0:T(1,128)} %get-tuple-element.8) | copy-start | bytes 24580

commit v3 on v2

--- a/solution.py
+++ b/solution.py
@@ -24,8 +24,9 @@
 def kernel(
     sizes, noise_ref, data_ref, out_ref, np_ref, dpot_ref,
     nz, dat, scores, w, vcol, lcol, ubuf, lbuf, ybuf, blane, fbuf,
-    pk, csend, cbuf, xsend, xbuf, zsend, zbuf,
+    pk, csend, cbuf, xsend, xbuf, zsend, zbuf, pdat, pscores, pv, pw,
     sent, dsem, zout, zsem, xsem, csem, lsem, ysem, fsem, rcsem, rxsem, rzsem,
+    psem, qsem, vsem,
 ):
     Z, total_rows, total_cols = sizes
     piece, D = noise_ref.shape
@@ -40,6 +41,7 @@
     id_y = (z * 2 + (1 - y), d)
     id_x = (n, (1 - x) * 2 + c)
     id_c = (n, x * 2 + (1 - c))
+    id_pair = ((z + 1 - 2 * (z % 2)) * 2 + y, d)
 
     def remote(src, dst, send_sem, recv_sem, device):
         return pltpu.make_async_remote_copy(
@@ -47,7 +49,7 @@
             device_id=device, device_id_type=MESH,
         )
 
-    X, C, L, Y, F, RC, RX, RZ, DATA = range(9)
+    X, C, L, Y, F, RC, RX, RZ, DATA, PAIR, PAIR_Y, V = range(12)
 
     group = [(zo, do) for zo in range(Z) for do in range(4) if (zo, do) != (0, 0)]
 
@@ -147,6 +149,23 @@
     remote(dat.at[1 - y], dat.at[1 - y], sent.at[DATA], dsem.at[0], id_y).wait_recv()
     lcol[pl.ds(pl.multiple_of((1 - y) * dpiece, dpiece), dpiece), :] = lane_sums(dat.at[1 - y])
 
+    quarter = dpiece // 4
+
+    def pair_copy(q):
+        at = pl.ds(q * quarter, quarter)
+        return remote(data_ref.at[at], pdat.at[y, at], sent.at[PAIR], psem.at[q], id_pair)
+
+    def pair_copy_y(q):
+        at = pl.ds(q * quarter, quarter)
+        return remote(pdat.at[y, at], pdat.at[y, at], sent.at[PAIR_Y], qsem.at[0], id_y)
+
+    for q in range(4):
+        pair_copy(q).start()
+
+    def forward(q):
+        pair_copy(q).wait_recv()
+        pair_copy_y(q).start()
+
     scale = 2.0 * LOG2E / (D * smoothing)
     norm_scale = LOG2E / (D * smoothing)
 
@@ -164,7 +183,17 @@
         -norm_scale * jnp.sum(lcol[...], axis=1, keepdims=True), (cols, 128)
     )
 
-    def row_lse(r):
+    def target(k):
+        return (z + 2 * k) % Z
+
+    def pair_product(yy):
+        for k in range(Z // 2):
+            pscores[k, pl.ds(pl.multiple_of(yy * dpiece, dpiece), dpiece), :] = scale * lax.dot_general(
+                pdat[yy], nz[target(k)].reshape(rows, D), (((1,), (1,)), ((), ())),
+                preferred_element_type=jnp.float32,
+            )
+
+    def row_lse(r, between=lambda: None):
         me = z * 4 + d
         for start in range(0, Z * rows, 128):
             t = scores[:, start : start + 128] + vcol[...]
@@ -173,6 +202,7 @@
             lbuf[r, me, :, start : start + 128] = top + jnp.log2(total)
         for zo, do in group:
             remote(lbuf.at[r, me], lbuf.at[r, me], sent.at[L], lsem.at[r], member(zo, do)).start()
+        between()
         others = lbuf.at[r, 0 : 4 * Z - 1]
         remote(others, others, sent.at[L], lsem.at[r], id_c).wait_recv()
         parts = [lbuf[r, s] for s in range(4 * Z)]
@@ -184,7 +214,7 @@
         top = jnp.maximum(a, b)
         return top + jnp.log2(exp2(a - top) + exp2(b - top))
 
-    def column_lse(r):
+    def column_lse(r, between=lambda: None):
         chunk = 64 if cols % 64 == 0 else cols
         for start in range(0, cols, chunk):
             t = scores[start : start + chunk, :] + ubuf[...]
@@ -195,16 +225,19 @@
             )
         ybuf[r, y] = jnp.transpose(lcol[...])[0:1, :]
         remote(ybuf.at[r, y], ybuf.at[r, y], sent.at[Y], ysem.at[r], id_y).start()
+        between()
         remote(ybuf.at[r, 1 - y], ybuf.at[r, 1 - y], sent.at[Y], ysem.at[r], id_y).wait_recv()
         lane = pair_lse(ybuf[r, 0], ybuf[r, 1])
         vcol[...] = jnp.transpose(jnp.broadcast_to(-math.log2(total_cols) - lane, (128, cols)))
         return lane
 
     for it in range(ITERS):
-        lse = row_lse(it)
+        lse = row_lse(it, (lambda: forward(2)) if it == 2 else (lambda: None))
         ubuf[...] = -math.log2(total_rows) - lse
-        lane = column_lse(it)
-
+        lane = column_lse(it, functools.partial(forward, (0, 1, 3)[it]))
+
+    pv[0] = -math.log2(total_cols) - lane
+    remote(pv.at[0], pv.at[1], sent.at[V], vsem.at[0], id_pair).start()
     fbuf[z] = -smoothing * math.log(total_cols) - (smoothing / LOG2E) * lane + blane[...] / D
     for zo in range(1, Z):
         remote(fbuf.at[z], fbuf.at[z], sent.at[F], fsem.at[0], member(zo, 0)).start()
@@ -216,20 +249,32 @@
         + own_norms / D
     )
 
-    ubuf[...] = row_lse(ITERS)
-    for b in range(Z):
+    ubuf[...] = row_lse(ITERS, lambda: pair_product(y))
+    theirs = pdat.at[1 - y]
+    remote(theirs, theirs, sent.at[PAIR_Y], qsem.at[0], id_y).wait_recv()
+    pair_product(1 - y)
+    for k in range(Z // 2):
         for start in range(0, rows, 128):
-            at = b * rows + start
-            t = scores[:, at : at + 128] + vcol[...] - ubuf[:, at : at + 128]
-            w[b, start : start + 128, :] = jnp.transpose(exp2(t)).astype(jnp.bfloat16)
+            at = pl.ds(pl.multiple_of(target(k) * rows + start, 128), 128)
+            t = scores[:, at] + vcol[...] - ubuf[:, at]
+            w[k, start : start + 128, :] = jnp.transpose(exp2(t)).astype(jnp.bfloat16)
+    remote(pv.at[1], pv.at[1], sent.at[V], vsem.at[0], id_pair).wait_recv()
+    vcol[...] = jnp.transpose(jnp.broadcast_to(pv[1], (128, cols)))
+    for k in range(Z // 2):
+        for start in range(0, rows, 128):
+            at = pl.ds(pl.multiple_of(target(k) * rows + start, 128), 128)
+            t = pscores[k, :, start : start + 128] + vcol[...] - ubuf[:, at]
+            pw[k, start : start + 128, :] = jnp.transpose(exp2(t)).astype(jnp.bfloat16)
 
     part = rows // 2
 
-    def block(b, h, column):
+    def block(k, h, column):
+        at = pl.ds(pl.multiple_of(column * width, width), width)
+        lines = slice(h * part, (h + 1) * part)
         return jnp.dot(
-            w[b, h * part : (h + 1) * part, :],
-            dat[:, :, pl.ds(pl.multiple_of(column * width, width), width)].reshape(cols, width),
-            preferred_element_type=jnp.float32,
+            w[k, lines, :], dat[:, :, at].reshape(cols, width), preferred_element_type=jnp.float32
+        ) + jnp.dot(
+            pw[k, lines, :], pdat[:, :, at].reshape(cols, width), preferred_element_type=jnp.float32
         )
 
     def core_copy(off, h, far):
@@ -241,15 +286,14 @@
         return remote(xsend.at[off, h], xbuf.at[off, h], sent.at[RX], rxsem.at[off, h], id_x)
 
     def z_copy(off, h):
-        return remote(zsend.at[off - 1, h], zbuf.at[off - 1, h], sent.at[RZ], rzsem.at[0], member(off, 0))
+        return remote(zsend.at[off - 1, h], zbuf.at[off - 1, h], sent.at[RZ], rzsem.at[0], member(2 * off, 0))
 
     def products(off, h):
-        b = (z + off) % Z
         for far in (1, 0):
             side = 1 - x if far else x
-            csend[off, far, h] = block(b, h, side * 2 + (1 - c))
+            csend[off, far, h] = block(off, h, side * 2 + (1 - c))
             core_copy(off, h, far).start()
-            pk[off, far, h] = block(b, h, side * 2 + c)
+            pk[off, far, h] = block(off, h, side * 2 + c)
 
     def send_x(off, h):
         core_copy(off, h, 1).wait_recv()
@@ -266,7 +310,7 @@
         else:
             pk[0, 0, h] = total
 
-    offsets = [Z // 2] + [o for o in range(1, Z) if o != Z // 2] + [0]
+    offsets = list(range(1, Z // 2)) + [0]
     order = [(off, h) for off in offsets for h in range(2)]
     for place in range(len(order) + 3):
         if place < len(order):
@@ -281,7 +325,7 @@
     remote(zbuf, zbuf, sent.at[RZ], rzsem.at[0], id_c).wait_recv()
     for h in range(2):
         total = pk[0, 0, h]
-        for off in range(1, Z):
+        for off in range(1, Z // 2):
             total = total + zbuf[off - 1, h].astype(jnp.float32)
         out_ref[h * part : (h + 1) * part, :] = total.astype(jnp.bfloat16)
 
@@ -298,6 +342,9 @@
     remote(ybuf.at[:, 0], ybuf.at[:, 0], sent.at[Y], ysem.at[0], id_y).wait_send()
     others = fbuf.at[0 : Z - 1]
     remote(others, others, sent.at[F], fsem.at[0], id_c).wait_send()
+    remote(data_ref, pdat.at[y], sent.at[PAIR], psem.at[0], id_pair).wait_send()
+    remote(pdat.at[0], pdat.at[0], sent.at[PAIR_Y], qsem.at[0], id_y).wait_send()
+    remote(pv.at[0], pv.at[1], sent.at[V], vsem.at[0], id_pair).wait_send()
     remote(csend, cbuf, sent.at[RC], rcsem.at[0, 0, 0], id_c).wait_send()
     remote(xsend, xbuf, sent.at[RX], rxsem.at[0, 0], id_x).wait_send()
     remote(zsend, zbuf, sent.at[RZ], rzsem.at[0], id_c).wait_send()
@@ -311,7 +358,7 @@
         ((Z, 4, piece, D), bf16),
         ((2, dpiece, D), bf16),
         ((cols, Z * rows), f32),
-        ((Z, rows, cols), bf16),
+        ((Z // 2, rows, cols), bf16),
         ((cols, 128), f32),
         ((cols, 128), f32),
         ((1, Z * rows), f32),
@@ -319,15 +366,19 @@
         ((ITERS, 2, 1, cols), f32),
         ((1, cols), f32),
         ((Z, 1, cols), f32),
-        ((Z, 2, 2, part, width), f32),
-        ((Z, 2, 2, part, width), f32),
-        ((Z, 2, 2, part, width), f32),
-        ((Z, 2, part, width), bf16),
-        ((Z, 2, part, width), bf16),
-        ((Z - 1, 2, part, width), bf16),
-        ((Z - 1, 2, part, width), bf16),
+        ((Z // 2, 2, 2, part, width), f32),
+        ((Z // 2, 2, 2, part, width), f32),
+        ((Z // 2, 2, 2, part, width), f32),
+        ((Z // 2, 2, part, width), bf16),
+        ((Z // 2, 2, part, width), bf16),
+        ((Z // 2 - 1, 2, part, width), bf16),
+        ((Z // 2 - 1, 2, part, width), bf16),
+        ((2, dpiece, D), bf16),
+        ((Z // 2, cols, rows), f32),
+        ((2, 1, cols), f32),
+        ((Z // 2, rows, cols), bf16),
     ]
-    sems = [(9,), (1,), (2, Z), (2, Z), (2, Z), (1,), (ITERS + 1,), (ITERS,), (1,), (Z, 2, 2), (Z, 2), (1,)]
+    sems = [(12,), (1,), (2, Z), (2, Z), (2, Z), (1,), (ITERS + 1,), (ITERS,), (1,), (Z // 2, 2, 2), (Z // 2, 2), (1,), (4,), (1,), (1,)]
     return arrays, sems
 
 
@@ -390,7 +441,7 @@
         devices = noise_size * dp_size
         totals = (piece * devices, dpiece * devices)
         Z = noise_size // 2
-        fits = noise_size % 2 == 0 and dp_size == 4 and Z >= 2
+        fits = noise_size % 2 == 0 and dp_size == 4 and Z >= 4 and Z % 2 == 0 and dpiece % 64 == 0
         if fits:
             arrays = scratch(Z, piece, dpiece, D)[0]
             fits = sum(math.prod(s) * jnp.dtype(t).itemsize for s, t in arrays) < VMEM_LIMIT * 3 // 4

time: 104 us -> 115 us (1.11)
  Pallas kernels: 100 us -> 111 us
    pallas_call x1, Pallas kernels: 100 us -> 111 us  [tiled_local(): pl.pallas_call(functools.partial(kernel, (Z, total_rows, total_cols)), ou...]
where the time goes in v3:
time: 115 us; the launch traced here: 114 us
  Pallas kernels  111 us (97%)
  local copies, waits for them, and re-layouts  2.85 us (2%)
    pallas_call x1, Pallas kernels, tiled_local(): pl.pallas_call(functools.partial(kernel, (Z, total_rows, total_cols)), ou...  111 us
    unnamed x7, local copies, waits for them, and re-layouts  2.85 us

profile of v3, /device:TPU:0, one launch (start us, length us, event | category | flops | bytes accessed | tf_op | source)
XLA Modules:
  0.0 114.3 jit_solution(11298384632852656814)
XLA Ops:
  0.6 110.8 %shard_map.49 = (bf16[256,512]{1,0:T(8,128)(2,1)}, f32[1,256]{1,0:T(1,128)}, f32[4,1,512]{2,1,0:T(1,128)}) custom-call(bf16[64,2048]{1,0:T(8,128)(2,1)} %noise_ref.1, bf16[256,2048]{1,0:T(8,128)(2,1)} %data_ref.1), custom_call_target="tpu_custom_call" | custom-call | tf_op jit(solution)/shard_map/pallas_call | solution.py:391
  111.5 0.0 copy-start.1
  111.5 0.0 copy-start
  111.5 1.7 %copy.8 = bf16[256,512]{1,0:T(8,128)(2,1)} copy(bf16[256,512]{1,0:T(8,128)(2,1)} %get-tuple-element.12) | data formatting | bytes 524288
  113.2 0.0 copy-done.1
  113.2 0.6 copy.9
  113.7 0.0 copy-done
  113.7 0.6 copy.10
Async XLA Ops:
  111.5 1.7 %copy-start.1 = (f32[1,256]{1,0:T(1,128)S(1)}, f32[1,256]{1,0:T(1,128)}, u32[]{:S(2)}) copy-start(f32[1,256]{1,0:T(1,128)} %get-tuple-element.7) | copy-start | bytes 3076
  111.5 2.3 %copy-start = (f32[4,1,512]{2,1,0:T(1,128)S(1)}, f32[4,1,512]{2,1,0:T(1,128)}, u32[]{:S(2)}) copy-start(f32[4,1,512]{2,1,0:T(1,128)} %get-tuple-element.8) | copy-start | bytes 24580

commit v4 on v3

--- a/solution.py
+++ b/solution.py
@@ -15,6 +15,18 @@
 LOG2E = math.log2(math.e)
 MESH = pl.DeviceIdType.MESH
 VMEM_LIMIT = 56 * 1024 * 1024
+CHUNKS = 8
+FETCH = {
+    "start": ((0,), ()),
+    "row 0": ((1, 2), (0,)),
+    "column 0": ((3,), (1,)),
+    "after column 0": ((), (2,)),
+    "row 1": ((4, 5), (3,)),
+    "column 1": ((6,), (4,)),
+    "after column 1": ((), (5,)),
+    "row 2": ((7,), (6,)),
+    "column 2": ((), (7,)),
+}
 
 
 def exp2(a):
@@ -149,7 +161,7 @@
     remote(dat.at[1 - y], dat.at[1 - y], sent.at[DATA], dsem.at[0], id_y).wait_recv()
     lcol[pl.ds(pl.multiple_of((1 - y) * dpiece, dpiece), dpiece), :] = lane_sums(dat.at[1 - y])
 
-    quarter = dpiece // 4
+    quarter = dpiece // CHUNKS
 
     def pair_copy(q):
         at = pl.ds(q * quarter, quarter)
@@ -159,12 +171,15 @@
         at = pl.ds(q * quarter, quarter)
         return remote(pdat.at[y, at], pdat.at[y, at], sent.at[PAIR_Y], qsem.at[0], id_y)
 
-    for q in range(4):
-        pair_copy(q).start()
-
-    def forward(q):
-        pair_copy(q).wait_recv()
-        pair_copy_y(q).start()
+    def fetch(point):
+        out, onward = FETCH.get(point, ((), ()))
+        for q in out:
+            pair_copy(q).start()
+        for q in onward:
+            pair_copy(q).wait_recv()
+            pair_copy_y(q).start()
+
+    fetch("start")
 
     scale = 2.0 * LOG2E / (D * smoothing)
     norm_scale = LOG2E / (D * smoothing)
@@ -232,9 +247,11 @@
         return lane
 
     for it in range(ITERS):
-        lse = row_lse(it, (lambda: forward(2)) if it == 2 else (lambda: None))
+        lse = row_lse(it, lambda: fetch(f"row {it}"))
+        fetch(f"after row {it}")
         ubuf[...] = -math.log2(total_rows) - lse
-        lane = column_lse(it, functools.partial(forward, (0, 1, 3)[it]))
+        lane = column_lse(it, lambda: fetch(f"column {it}"))
+        fetch(f"after column {it}")
 
     pv[0] = -math.log2(total_cols) - lane
     remote(pv.at[0], pv.at[1], sent.at[V], vsem.at[0], id_pair).start()
@@ -249,7 +266,11 @@
         + own_norms / D
     )
 
-    ubuf[...] = row_lse(ITERS, lambda: pair_product(y))
+    def last():
+        fetch(f"row {ITERS}")
+        pair_product(y)
+
+    ubuf[...] = row_lse(ITERS, last)
     theirs = pdat.at[1 - y]
     remote(theirs, theirs, sent.at[PAIR_Y], qsem.at[0], id_y).wait_recv()
     pair_product(1 - y)
@@ -378,7 +399,7 @@
         ((2, 1, cols), f32),
         ((Z // 2, rows, cols), bf16),
     ]
-    sems = [(12,), (1,), (2, Z), (2, Z), (2, Z), (1,), (ITERS + 1,), (ITERS,), (1,), (Z // 2, 2, 2), (Z // 2, 2), (1,), (4,), (1,), (1,)]
+    sems = [(12,), (1,), (2, Z), (2, Z), (2, Z), (1,), (ITERS + 1,), (ITERS,), (1,), (Z // 2, 2, 2), (Z // 2, 2), (1,), (CHUNKS,), (1,), (1,)]
     return arrays, sems
 
 
@@ -441,7 +462,7 @@
         devices = noise_size * dp_size
         totals = (piece * devices, dpiece * devices)
         Z = noise_size // 2
-        fits = noise_size % 2 == 0 and dp_size == 4 and Z >= 4 and Z % 2 == 0 and dpiece % 64 == 0
+        fits = noise_size % 2 == 0 and dp_size == 4 and Z >= 4 and Z % 2 == 0 and dpiece % (16 * CHUNKS) == 0
         if fits:
             arrays = scratch(Z, piece, dpiece, D)[0]
             fits = sum(math.prod(s) * jnp.dtype(t).itemsize for s, t in arrays) < VMEM_LIMIT * 3 // 4

time: 115 us -> 96.4 us (0.84)
  Pallas kernels: 111 us -> 92.7 us
    pallas_call x1, Pallas kernels: 111 us -> 92.7 us  [tiled_local(): pl.pallas_call(functools.partial(kernel, (Z, total_rows, total_cols)), ou...]
where the time goes in v4:
time: 96.4 us; the launch traced here: 96.2 us
  Pallas kernels  92.7 us (96%)
  local copies, waits for them, and re-layouts  2.85 us (3%)
    pallas_call x1, Pallas kernels, tiled_local(): pl.pallas_call(functools.partial(kernel, (Z, total_rows, total_cols)), ou...  92.7 us
    unnamed x7, local copies, waits for them, and re-layouts  2.85 us

profile of v4, /device:TPU:0, one launch (start us, length us, event | category | flops | bytes accessed | tf_op | source)
XLA Modules:
  0.0 96.2 jit_solution(5667802745756433938)
XLA Ops:
  0.6 92.7 %shard_map.49 = (bf16[256,512]{1,0:T(8,128)(2,1)}, f32[1,256]{1,0:T(1,128)}, f32[4,1,512]{2,1,0:T(1,128)}) custom-call(bf16[64,2048]{1,0:T(8,128)(2,1)} %noise_ref.1, bf16[256,2048]{1,0:T(8,128)(2,1)} %data_ref.1), custom_call_target="tpu_custom_call" | custom-call | tf_op jit(solution)/shard_map/pallas_call | solution.py:412
  93.3 0.0 copy-start.1
  93.4 0.0 copy-start
  93.4 1.7 %copy.8 = bf16[256,512]{1,0:T(8,128)(2,1)} copy(bf16[256,512]{1,0:T(8,128)(2,1)} %get-tuple-element.12) | data formatting | bytes 524288
  95.0 0.0 copy-done.1
  95.0 0.6 copy.9
  95.6 0.0 copy-done
  95.6 0.6 copy.10
Async XLA Ops:
  93.3 1.7 %copy-start.1 = (f32[1,256]{1,0:T(1,128)S(1)}, f32[1,256]{1,0:T(1,128)}, u32[]{:S(2)}) copy-start(f32[1,256]{1,0:T(1,128)} %get-tuple-element.7) | copy-start | bytes 3076
  93.4 2.3 %copy-start = (f32[4,1,512]{2,1,0:T(1,128)S(1)}, f32[4,1,512]{2,1,0:T(1,128)}, u32[]{:S(2)}) copy-start(f32[4,1,512]{2,1,0:T(1,128)} %get-tuple-element.8) | copy-start | bytes 24580
